TPU v7x, 256 devices: a whole 4x4x8 slice. The times are simulated.
256 devices in a mesh: img: 16 (over z_lo, x, core), ref: 16 (over z_hi, y).
Axes of the slice: x: 4, y: 4, z: 8 (z_hi: 4, z_lo: 2; z = z_hi * 2 + z_lo), core: 2. Of those that a mesh axis runs over, the one named last changes fastest.
Arguments:
- images: bfloat16 [8192, 16384], P('img', 'ref'), may hold values from -24 to 24
- refs: bfloat16 [6912, 16384], P('ref', 'img'), may hold values from -0.0859375 to 0.0859375
- ctf: float32 [16, 16384], replicated, may hold values from 0.1 to 1
- ctf_group: int32 [8192], P('img'), may hold values from 0 to 15
- class_id: int32 [6912], P('ref'), may hold values from 0 to 191
- rot_id: int32 [6912], P('ref'), may hold values from 0 to 35
- class_prior: float32 [192], replicated, may hold values from -1 to 1
- rot_prior: float32 [36], replicated, may hold values from -1 to 1
Outputs:
- class_avg: float32 [192, 16384], P('img', 'ref')
- occupancy: float32 [192], replicated
- log_evidence: float32 [8192], P('img')
All inputs are finite; a program needn't handle non-finite values.
Results may differ from a plain program's by a relative error of at most 0.0029.
Values may be sent and summed in bfloat16 or wider, within the bound.
No kernel may reach another device: no remote copies, remote signals or barrier semaphores. Data moves between devices by JAX's collectives and lax.ppermute only.
A program may use at most 128 MiB of HBM per device.

v0:
```python
import jax
import jax.numpy as jnp
from jax import lax
from jax.sharding import PartitionSpec as P

NCLASS = 192
NROT = 36


def body(images, refs, ctf, ctf_group, class_id, rot_id, class_prior, rot_prior):
    highest = lax.Precision.HIGHEST
    contract_last = (((1,), (1,)), ((), ()))
    img_rows = images.shape[0]
    ref_rows = refs.shape[0]
    image_width = images.shape[1]
    group_count = ctf.shape[0]
    group_hot = (ctf_group[:, None] == jnp.arange(group_count, dtype=jnp.int32)[None, :]).astype(
        jnp.float32
    )
    ctf_slab = lax.dynamic_slice_in_dim(ctf, lax.axis_index("ref") * image_width, image_width, 1)
    ctf_rows = jnp.dot(group_hot, ctf_slab, precision=highest)
    weighted = (ctf_rows * images.astype(jnp.float32)).astype(jnp.bfloat16)
    gathered = lax.all_gather(weighted, "ref", axis=1, tiled=True)
    ctf_square = ctf * ctf
    score_init = jnp.zeros((img_rows, ref_rows), jnp.float32)
    norm_init = jnp.zeros((group_count, ref_rows), jnp.float32)
    portion = lax.all_gather(refs, "img", axis=1, tiled=True)
    score_acc = lax.dot_general(
        gathered, portion, contract_last, preferred_element_type=jnp.float32
    )
    score_acc, norm_acc = (score_acc, (score_init, norm_init)[1])
    squared = portion.astype(jnp.float32) * portion.astype(jnp.float32)
    norm_acc = lax.dot_general(ctf_square, squared, contract_last, precision=highest)
    score_acc, norms = (score_acc, norm_acc)
    class_match = class_id[:, None] == jnp.arange(NCLASS, dtype=jnp.int32)[None, :]
    rot_match = rot_id[:, None] == jnp.arange(NROT, dtype=jnp.int32)[None, :]
    priors = jnp.sum(jnp.where(class_match, class_prior[None, :], 0.0), axis=1) + jnp.sum(
        jnp.where(rot_match, rot_prior[None, :], 0.0), axis=1
    )
    offsets = priors[None, :] - 0.5 * norms
    scores = score_acc + jnp.dot(group_hot, offsets, precision=highest)
    row_top = lax.pmax(jnp.max(scores, axis=1), "ref")
    row_sum = lax.psum(jnp.sum(jnp.exp(scores - row_top[:, None]), axis=1), "ref")
    evidence = row_top + jnp.log(row_sum)
    posterior = jnp.exp(scores - evidence[:, None])
    class_part = jnp.dot(posterior, class_match.astype(jnp.float32), precision=highest)
    class_post = lax.psum(class_part, "ref")
    counts = lax.psum(jnp.sum(class_post, axis=0), "img")
    post_weights = class_post.astype(jnp.bfloat16)
    contract_first = (((0,), (0,)), ((), ()))
    owned = NCLASS // lax.axis_size("img")
    first_class = lax.axis_index("img") * owned
    every_sum = lax.psum(
        lax.dot_general(post_weights, images, contract_first, preferred_element_type=jnp.float32),
        "img",
    )
    own_sums = lax.dynamic_slice_in_dim(every_sum, first_class, owned, 0)
    own_counts = lax.dynamic_slice_in_dim(counts, first_class, owned, 0)
    class_avg = own_sums / (own_counts[:, None] + 1.0)
    occupancy = counts * (NCLASS / (img_rows * lax.axis_size("img")))
    return (class_avg, occupancy, evidence)


def solution(mesh):
    placed = (P("img", "ref"), P("ref", "img"), P(), P("img"), P("ref"), P("ref"), P(), P())
    return jax.shard_map(
        body,
        mesh=mesh,
        in_specs=placed,
        out_specs=(P("img", "ref"), P(), P("img")),
        check_vma=False,
    )
```

profile of v0, /device:TPU:1, one launch (start us, length us, event | category | flops | bytes accessed | tf_op | source)
XLA Modules:
  0.0 695.9 jit_solution(6234549893179064225)
XLA Ops:
  7.2 0.7 all-gather.5.cloned.1.call-update
  7.9 0.0 all-gather.3.cloned.1.call-start
  8.0 3.3 multiply_convert_fusion
  11.3 0.0 all-reduce.3.cloned.1.call-start
  11.4 0.8 select_reduce_fusion.1
  12.2 0.8 select_reduce_fusion
  13.0 83.0 %all-gather.5.cloned.1.call-done = bf16[432,16384]{1,0:T(8,128)(2,1)} async-done(((bf16[432,1024]{1,0:T(8,128)(2,1)}), bf16[432,16384]{1,0:T(8,128)(2,1)}) %all-gather.5.cloned.1.call-update) | async-done | bytes 14155792 | tf_op jit(solution)/shard_map/all_gather | solution.py:27
  96.0 26.0 %fusion.6 = f32[16,432]{1,0:T(8,128)S(1)} fusion(bf16[432,16384]{1,0:T(8,128)(2,1)} %all-gather.5.cloned.1.call-done, f32[16,16384]{1,0:T(8,128)} %param.10, f32[432]{0:T(512)S(1)} %add.33), kind=kOutput, calls=%fused_computation.6 | convolution fusion | flops 1373386240 | bytes 15233728 | tf_op jit(solution)/shard_map/dot_general | solution.py:33
  122.0 0.6 fusion.14
  122.6 178.1 %all-gather.3.cloned.1.call-done = bf16[512,16384]{1,0:T(8,128)(2,1)} async-done(((bf16[512,1024]{1,0:T(8,128)(2,1)}), bf16[512,16384]{1,0:T(8,128)(2,1)}) %all-gather.3.cloned.1.call-update) | async-done | bytes 16777232 | tf_op jit(solution)/shard_map/all_gather | solution.py:23
  300.7 15.3 %fusion.22 = (f32[512]{0:T(512)S(1)}, f32[512,432]{0,1:T(8,128)S(1)}) fusion(f32[512,432]{0,1:T(8,128)S(1)} %fusion.14, bf16[512,16384]{1,0:T(8,128)(2,1)} %all-gather.3.cloned.1.call-done, bf16[432,16384]{1,0:T(8,128)(2,1)} %all-gather.5.cloned.1.call-done), kind=kOutput, calls=%fused_computation.30 | convolution fusion | flops 7248199168 | bytes 32704512 | tf_op jit(solution)/shard_map/dot_general | solution.py:28
  316.0 37.7 %pmax.7 = f32[512]{0:T(512)S(1)} all-reduce(f32[512]{0:T(512)S(1)} %get-tuple-element.3), channel_id=1, replica_groups=mesh['img'=16,'ref'=16] {'ref'}, use_global_device_ids=true, to_apply=%region_3.4 | all-reduce | flops 512 | bytes 4096 | tf_op jit(solution)/shard_map/pmax | solution.py:42
  353.7 0.2 exponential_reduce_fusion
  353.8 32.1 %psum.28 = f32[512]{0:T(512)S(1)} all-reduce(f32[512]{0:T(512)S(1)} %exponential_reduce_fusion), channel_id=1, replica_groups=mesh['img'=16,'ref'=16] {'ref'}, use_global_device_ids=true, to_apply=%region_5.6 | all-reduce | flops 512 | bytes 4096 | tf_op jit(solution)/shard_map/psum | solution.py:43
  386.0 1.4 fusion.10
  387.4 0.0 all-reduce.5.cloned.1.call-start
  387.5 165.6 %all-reduce.3.cloned.1.call-done = f32[512,192]{0,1:T(8,128)} async-done(((f32[512,192]{0,1:T(8,128)}), f32[512,192]{0,1:T(8,128)}) %all-reduce.3.cloned.1.call-update) | async-done | bytes 393232 | tf_op jit(solution)/shard_map/psum | solution.py:47
  553.1 2.3 fusion.15
  555.4 1.1 reduce_sum.39
  556.5 37.7 %psum.31 = f32[192]{0:T(256)S(1)} all-reduce(f32[192]{0:T(256)S(1)} %reduce_sum.39), channel_id=1, replica_groups=mesh['img'=16,'ref'=16] {'img'}, use_global_device_ids=true, to_apply=%region_9.10 | all-reduce | flops 192 | bytes 1536 | tf_op jit(solution)/shard_map/psum | solution.py:48
  594.2 0.1 dynamic-slice_add_fusion
  594.3 0.6 broadcast_multiply_fusion
  594.8 92.9 %all-reduce.5.cloned.1.call-done = f32[192,1024]{1,0:T(8,128)} async-done(((f32[192,1024]{1,0:T(8,128)}), f32[192,1024]{1,0:T(8,128)}) %all-reduce.5.cloned.1.call-update) | async-done | bytes 786448 | tf_op jit(solution)/shard_map/psum | solution.py:53
  687.7 1.6 dynamic-slice_divide_fusion
  (14 shorter events, 0.1 us)
Async XLA Ops:
  7.2 114.8 %copy-start.3 = (s32[512]{0:T(512)S(1)}, s32[512]{0:T(512)}, u32[]{:S(2)}) copy-start(s32[512]{0:T(512)} %param.11) | copy-start | bytes 6148
  7.2 88.8 %all-gather.5.cloned.1.call-start = ((), (), s32[]{:S(2)}) async-start(), calls=%async_computation.1 | async-start | bytes 15040512 | tf_op jit(solution)/shard_map/all_gather | solution.py:27
  7.9 292.8 %all-gather.3.cloned.1.call-start = ((), (), s32[]{:S(2)}) async-start(), calls=%async_computation | async-start | bytes 17825792 | tf_op jit(solution)/shard_map/all_gather | solution.py:23
  11.3 541.8 %all-reduce.3.cloned.1.call-start = ((), (), s32[]{:S(2)}) async-start(), calls=%async_computation.2 | async-start | bytes 786432 | tf_op jit(solution)/shard_map/psum | solution.py:47
  122.6 263.3 %copy-start.2 = (s32[432]{0:T(512)S(1)}, s32[432]{0:T(512)}, u32[]{:S(2)}) copy-start(s32[432]{0:T(512)} %param.12) | copy-start | bytes 5188
  122.6 430.5 %copy-start = (bf16[512,1024]{1,0:T(8,128)(2,1)S(1)}, bf16[512,1024]{1,0:T(8,128)(2,1)}, u32[]{:S(2)}) copy-start(bf16[512,1024]{1,0:T(8,128)(2,1)} %param.8) | copy-start | bytes 3145732
  385.9 303.4 %copy-start.1 = (f32[512]{0:T(512)}, f32[512]{0:T(512)S(1)}, u32[]{:S(2)}) copy-start(f32[512]{0:T(512)S(1)} %log_add_fusion) | copy-start | bytes 6148
  387.4 300.3 %all-reduce.5.cloned.1.call-start = ((), (), s32[]{:S(2)}) async-start(), calls=%async_computation.3 | async-start | bytes 1572864 | tf_op jit(solution)/shard_map/psum | solution.py:53
Sparse Core Ops, SparseCore 0:
  9.8 86.0 all-gather.4
  98.4 202.2 all-gather.2
  387.5 165.5 all-reduce.2
  555.7 131.9 all-reduce.4
where the time goes:
time: 696 us
  waiting for transfers between devices  520 us (75%)
  blocking collectives  107 us (15%)
  matrix products  48.9 us (7%)
  between operations  13.9 us (2%)
    all_gather x1, waiting for transfers between devices, body(): gathered = lax.all_gather(weighted, 'ref', axis=1, tiled=True)  178 us
    psum x1, waiting for transfers between devices, body(): class_post = lax.psum(class_part, 'ref')  166 us
    psum x1, waiting for transfers between devices, body(): lax.psum(lax.dot_general(post_weights, images, contract_first, preferred_...  92.9 us
    all_gather x1, waiting for transfers between devices, body(): portion = lax.all_gather(refs, 'img', axis=1, tiled=True)  83 us
    pmax x1, blocking collectives, body(): row_top = lax.pmax(jnp.max(scores, axis=1), 'ref')  37.7 us
    psum x1, blocking collectives, body(): counts = lax.psum(jnp.sum(class_post, axis=0), 'img')  37.7 us
    psum x1, blocking collectives, body(): lax.psum(jnp.sum(jnp.exp(scores - row_top[:, None]), axis=1), 'ref')  32.1 us
    dot_general x1, matrix products, body(): lax.dot_general(ctf_square, squared, contract_last, precision=highest)  26 us
  transfers between devices with their start and end apart: 4, of which 4 were waited for; matrix products, arithmetic and copies ran while one was open for 5% of the time, Pallas kernels for 0%

commit v1 on v0

v1 whole, which is shorter than its diff:
```python
import jax
import jax.numpy as jnp
from jax import lax
from jax.sharding import Mesh, PartitionSpec as P

NCLASS = 192
NROT = 36
HIGHEST = lax.Precision.HIGHEST
LAST = (((1,), (1,)), ((), ()))
FIRST = (((0,), (0,)), ((), ()))


def image_moves():
    moves = []
    for x in range(4):
        for h in range(4):
            for y in range(4):
                to_x = (h & 1) * 2 + (y >> 1)
                to_y = (h >> 1) * 2 + (y & 1)
                moves.append(((x * 4 + h) * 4 + y, (to_x * 4 + x) * 4 + to_y))
    return moves


def everywhere(block, axis, size):
    spread = jnp.broadcast_to(block[None], (size,) + block.shape)
    return lax.all_to_all(spread, axis, 0, 0, tiled=True)


def body(images, refs, ctf, ctf_group, class_id, rot_id, class_prior, rot_prior):
    rows, width = images.shape
    ref_rows = refs.shape[0]
    groups = ctf.shape[0]
    img_place = (lax.axis_index("a") * 4 + lax.axis_index("x")) * 2 + lax.axis_index("c")
    ref_place = lax.axis_index("h") * 4 + lax.axis_index("y")

    gathered = lax.all_gather(refs, ("a", "c", "h"), axis=0)

    group_hot = (ctf_group[:, None] == jnp.arange(groups, dtype=jnp.int32)[None, :]).astype(jnp.float32)
    ctf_slab = lax.dynamic_slice_in_dim(ctf, ref_place * width, width, 1)
    ctf_rows = jnp.dot(group_hot, ctf_slab, precision=HIGHEST)
    weighted = (ctf_rows * images.astype(jnp.float32)).astype(jnp.bfloat16)
    moves = image_moves()
    moved = lax.ppermute(weighted, ("x", "h", "y"), moves)
    moved_group = lax.ppermute(ctf_group, ("x", "h", "y"), moves)
    pieces = everywhere(moved, "y", 4)

    ref_slab = lax.dynamic_slice_in_dim(ctf, img_place * width, width, 1)
    ref_float = refs.astype(jnp.float32)
    norm_part = lax.dot_general(ref_slab * ref_slab, ref_float * ref_float, LAST, precision=HIGHEST)
    class_match = class_id[:, None] == jnp.arange(NCLASS, dtype=jnp.int32)[None, :]
    rot_match = rot_id[:, None] == jnp.arange(NROT, dtype=jnp.int32)[None, :]
    priors = jnp.sum(jnp.where(class_match, class_prior[None, :], 0.0), axis=1) + jnp.sum(
        jnp.where(rot_match, rot_prior[None, :], 0.0), axis=1
    )
    facts = jnp.concatenate(
        [norm_part, priors[None], class_id.astype(jnp.float32)[None], jnp.zeros((6, ref_rows), jnp.float32)], 0
    )
    all_facts = lax.all_gather(facts, ("a", "c", "h"), axis=0)
    all_facts = all_facts.reshape(4, 4, 24, ref_rows)
    norms = jnp.sum(all_facts[:, :, :groups], axis=0).transpose(1, 0, 2).reshape(groups, 4 * ref_rows)
    all_priors = all_facts[0, :, groups].reshape(4 * ref_rows)
    all_classes = all_facts[0, :, groups + 1].reshape(4 * ref_rows)

    moved_hot = (moved_group[:, None] == jnp.arange(groups, dtype=jnp.int32)[None, :]).astype(jnp.float32)
    scores = jnp.dot(moved_hot, -0.5 * norms, precision=HIGHEST)
    blocks = gathered.reshape(4, 4 * ref_rows, width)
    for j in range(4):
        scores = scores + lax.dot_general(pieces[j], blocks[j], LAST, preferred_element_type=jnp.float32)

    quarter = rows // 4
    parts = lax.all_to_all(scores.reshape(4, quarter, 4 * ref_rows), "x", 0, 0, tiled=True)
    own = jnp.sum(parts, axis=0) + all_priors[None, :]
    top = jnp.max(own, axis=1)
    class_hot = (all_classes[:, None] == jnp.arange(NCLASS, dtype=jnp.float32)[None, :]).astype(jnp.float32)
    class_part = jnp.dot(jnp.exp(own - top[:, None]), class_hot, precision=HIGHEST)
    payload = jnp.concatenate([class_part, jnp.broadcast_to(top[:, None], (quarter, 64))], axis=1)
    payload = everywhere(payload, "y", 4)
    tops = payload[:, :, NCLASS]
    row_top = jnp.max(tops, axis=0)
    mass = jnp.sum(payload[:, :, :NCLASS] * jnp.exp(tops - row_top[None])[:, :, None], axis=0)
    total = jnp.sum(mass, axis=1)
    evidence = row_top + jnp.log(total)
    posterior = mass / total[:, None]
    payload = jnp.concatenate([posterior, jnp.broadcast_to(evidence[:, None], (quarter, 64))], axis=1)
    swap = [(x * 4 + h, h * 4 + x) for x in range(4) for h in range(4)]
    payload = lax.ppermute(payload, ("x", "h"), swap)
    payload = everywhere(payload, "h", 4).reshape(rows, NCLASS + 64)
    class_post = payload[:, :NCLASS]
    log_evidence = payload[:, NCLASS]

    counts_part = jnp.sum(class_post, axis=0)
    sums_part = lax.dot_general(class_post.astype(jnp.bfloat16), images, FIRST, preferred_element_type=jnp.float32)
    owned = NCLASS // 16
    count_rows = jnp.broadcast_to(jnp.pad(counts_part, (0, width - NCLASS))[None, None], (16, 4, width))
    outgoing = jnp.concatenate([sums_part.reshape(16, owned, width), count_rows], axis=1)
    arrived = jnp.sum(lax.all_to_all(outgoing, ("a", "x", "c"), 0, 0, tiled=True), axis=0)
    counts = arrived[owned, :NCLASS]
    own_counts = lax.dynamic_slice_in_dim(counts, img_place * owned, owned, 0)
    class_avg = arrived[:owned] / (own_counts[:, None] + 1.0)
    occupancy = counts * (NCLASS / (rows * 16))
    return class_avg, occupancy, log_evidence


def solution(mesh):
    split = Mesh(mesh.devices.reshape(2, 4, 2, 4, 4), ("a", "x", "c", "h", "y"))
    img, ref = ("a", "x", "c"), ("h", "y")
    placed = (P(img, ref), P(ref, img), P(), P(img), P(ref), P(ref), P(), P())
    return jax.shard_map(
        body,
        mesh=split,
        in_specs=placed,
        out_specs=(P(img, ref), P(), P(img)),
        check_vma=False,
    )
```

time: 696 us -> 545 us (0.78)
  waiting for transfers between devices: 520 us -> 213 us
  starting transfers between devices: 0.16 us -> 102 us
  blocking collectives: 107 us -> 170 us
  matrix products: 48.9 us -> 28.9 us
  local copies, waits for them, and re-layouts: 0.02 us -> 9.45 us
    psum x2 -> x0, waiting for transfers between devices: 259 us -> none  [the longest x1 166 us: body(): class_post = lax.psum(class_part, 'ref')]
    all_gather x0 -> x1, blocking collectives: none -> 122 us  [body(): all_facts = lax.all_gather(facts, ('a', 'c', 'h'), axis=0)]
    all_gather x2 -> x1, waiting for transfers between devices: 261 us -> 161 us  [body(): gathered = lax.all_gather(refs, ('a', 'c', 'h'), axis=0)]
    all_to_all x0 -> x3, starting transfers between devices: none -> 100 us  [the longest x1 70.4 us: everywhere(): return lax.all_to_all(spread, axis, 0, 0, tiled=True)]
    psum x2 -> x0, blocking collectives: 69.8 us -> none  [the longest x1 37.7 us: body(): counts = lax.psum(jnp.sum(class_post, axis=0), 'img')]
    all_to_all x0 -> x3, waiting for transfers between devices: none -> 52.2 us  [the longest x1 37.1 us: body(): lax.all_to_all(scores.reshape(4, quarter, 4 * ref_rows), 'x', 0, 0, tiled...]
    all_to_all x0 -> x2, blocking collectives: none -> 47.3 us  [everywhere(): return lax.all_to_all(spread, axis, 0, 0, tiled=True)]
    pmax x1 -> x0, blocking collectives: 37.7 us -> none  [body(): row_top = lax.pmax(jnp.max(scores, axis=1), 'ref')]
  transfers between devices with their start and end apart: 4 -> 7, of which waited for: 4 -> 3; matrix products, arithmetic and copies ran while one was open for 5% -> 3% of each run, Pallas kernels for 0% -> 0%
where the time goes in v1:
time: 545 us; the launch traced here: 544 us
  waiting for transfers between devices  213 us (39%)
  blocking collectives  170 us (31%)
  starting transfers between devices  102 us (19%)
  matrix products  28.9 us (5%)
  between operations  14.4 us (3%)
  local copies, waits for them, and re-layouts  9.45 us (2%)
  other arithmetic  5.85 us (1%)
    all_gather x1, waiting for transfers between devices, body(): gathered = lax.all_gather(refs, ('a', 'c', 'h'), axis=0)  161 us
    all_gather x1, blocking collectives, body(): all_facts = lax.all_gather(facts, ('a', 'c', 'h'), axis=0)  122 us
    all_to_all x1, starting transfers between devices, everywhere(): return lax.all_to_all(spread, axis, 0, 0, tiled=True)  70.4 us
    all_to_all x2, blocking collectives, everywhere(): return lax.all_to_all(spread, axis, 0, 0, tiled=True)  47.3 us
    all_to_all x1, waiting for transfers between devices, body(): lax.all_to_all(scores.reshape(4, quarter, 4 * ref_rows), 'x', 0, 0, tiled...  37.1 us
    all_to_all x1, starting transfers between devices, body(): lax.all_to_all(scores.reshape(4, quarter, 4 * ref_rows), 'x', 0, 0, tiled...  24.8 us
    dot_general x4, matrix products, body(): lax.dot_general(pieces[j], blocks[j], LAST, preferred_element_type=jnp.fl...  17.9 us
    all_to_all x1, waiting for transfers between devices, body(): lax.all_to_all(outgoing, ('a', 'x', 'c'), 0, 0, tiled=True)  15.1 us
  transfers between devices with their start and end apart: 7, of which 3 were waited for; matrix products, arithmetic and copies ran while one was open for 3% of the time, Pallas kernels for 0%

profile of v1, /device:TPU:1, one launch (start us, length us, event | category | flops | bytes accessed | tf_op | source)
XLA Modules:
  0.0 543.9 jit_solution(1356710384544708398)
XLA Ops:
  7.9 2.3 multiply_convert_fusion
  11.0 2.6 broadcast_in_dim.46
  13.7 70.4 %all-to-all-start = ((bf16[4,512,1024]{2,1,0:T(8,128)(2,1)}), bf16[4,512,1024]{2,1,0:T(8,128)(2,1)}, u32[]{:S(2)}, u32[]{:S(2)}) async-start(bf16[4,512,1024]{2,1,0:T(8,128)(2,1)} %broadcast_in_dim.46), calls=%async_computation | async-start | bytes 8388608 | tf_op jit(solution)/shard_map/all_to_all | solution.py:26
  85.2 2.4 fusion.10
  87.6 122.4 %all-gather = f32[384,432]{1,0:T(8,128)S(1)} all-gather(f32[24,432]{1,0:T(8,128)S(1)} %maximum_maximum_fusion), channel_id=2, replica_groups=mesh['a'=2,'x'=4,'c'=2,'h'=4,'y'=4] {'a','c','h'}, dimensions={0}, use_global_device_ids=true | all-gather | bytes 705024 | tf_op jit(solution)/shard_map/all_gather | solution.py:58
  210.0 0.9 copy-done.2
  211.8 2.6 fusion.23
  214.4 160.5 %all-gather.4.cloned.1.call-done = bf16[6912,1024]{1,0:T(8,128)(2,1)} async-done(((bf16[432,1024]{1,0:T(8,128)(2,1)}), bf16[6912,1024]{1,0:T(8,128)(2,1)}) %all-gather.4.cloned.1.call-update) | async-done | bytes 14155792 | tf_op jit(solution)/shard_map/all_gather | solution.py:36
  374.9 4.4 fusion.2
  379.3 4.4 fusion.4
  383.7 4.4 fusion.6
  388.0 4.8 add_bitcast_fusion
  392.9 2.0 copy.26
  394.8 24.8 %all-to-all-start.1 = ((f32[4,128,1728]{1,2,0:T(8,128)}), f32[4,128,1728]{1,2,0:T(8,128)S(1)}, u32[]{:S(2)}, u32[]{:S(2)}) async-start(f32[4,128,1728]{1,2,0:T(8,128)} %bitcast.29), calls=%async_computation.1 | async-start | bytes 7077888 | tf_op jit(solution)/shard_map/all_to_all | solution.py:71
  419.6 1.0 slice_reduce_fusion.3
  421.3 37.1 %all-to-all-done.1 = f32[4,128,1728]{1,2,0:T(8,128)S(1)} async-done(((f32[4,128,1728]{1,2,0:T(8,128)}), f32[4,128,1728]{1,2,0:T(8,128)S(1)}, u32[]{:S(2)}, u32[]{:S(2)}) %all-to-all-start.1) | async-done | bytes 3538976 | tf_op jit(solution)/shard_map/all_to_all | solution.py:71
  458.4 1.2 reduce_sum.75
  459.6 1.5 add_reduce_fusion
  461.1 3.4 fusion.13
  464.6 13.7 %all_to_all.25 = f32[4,128,256]{1,2,0:T(8,128)S(1)} all-to-all(f32[4,128,256]{1,2,0:T(8,128)S(1)} %broadcast_in_dim.48), channel_id=1, replica_groups=mesh['a'=2,'x'=4,'c'=2,'h'=4,'y'=4] {'y'}, dimensions={0} | all-to-all | bytes 1048576 | tf_op jit(solution)/shard_map/all_to_all | solution.py:26
  479.3 33.6 %all_to_all.26 = f32[4,128,256]{1,2,0:T(8,128)S(1)} all-to-all(f32[4,128,256]{1,2,0:T(8,128)S(1)} %broadcast_in_dim.50), channel_id=1, replica_groups=mesh['a'=2,'x'=4,'c'=2,'h'=4,'y'=4] {'h'}, dimensions={0} | all-to-all | bytes 1048576 | tf_op jit(solution)/shard_map/all_to_all | solution.py:26
  513.7 1.1 pad_maximum_fusion
  514.8 5.0 all-to-all-start.4
  520.6 15.1 %all-to-all-done.4 = f32[16,16,1024]{2,1,0:T(8,128)S(1)} async-done(((f32[16,16,1024]{2,1,0:T(8,128)}), f32[16,16,1024]{2,1,0:T(8,128)S(1)}, u32[]{:S(2)}, u32[]{:S(2)}) %all-to-all-start.4) | async-done | bytes 1048608 | tf_op jit(solution)/shard_map/all_to_all | solution.py:96
  (61 shorter events, 8.2 us)
Async XLA Ops:
  7.2 367.8 %all-gather.4.cloned.1.call-start = ((), (), s32[]{:S(2)}) async-start(), calls=%async_computation.5 | async-start | bytes 15040512 | tf_op jit(solution)/shard_map/all_gather | solution.py:36
  10.3 0.7 collective-permute-start.1
  13.6 70.5 %copy-start.6 = (s32[512]{0:T(512)S(1)}, s32[512]{0:T(512)}, u32[]{:S(2)}) copy-start(s32[512]{0:T(512)} %param.11) | copy-start | bytes 6148
  13.6 71.2 %copy-start.4 = (s32[432]{0:T(512)S(1)}, s32[432]{0:T(512)}, u32[]{:S(2)}) copy-start(s32[432]{0:T(512)} %param.12) | copy-start | bytes 5188
  13.6 71.3 %copy-start.5 = (s32[432]{0:T(512)S(1)}, s32[432]{0:T(512)}, u32[]{:S(2)}) copy-start(s32[432]{0:T(512)} %param.13) | copy-start | bytes 5188
  13.6 71.3 %copy-start.8 = (f32[36]{0:T(128)S(1)}, f32[36]{0:T(128)}, u32[]{:S(2)}) copy-start(f32[36]{0:T(128)} %param.15) | copy-start | bytes 436
  13.7 71.3 %copy-start.7 = (f32[192]{0:T(256)S(1)}, f32[192]{0:T(256)}, u32[]{:S(2)}) copy-start(f32[192]{0:T(256)} %param.14) | copy-start | bytes 2308
  13.7 71.5 %copy-start.1 = (bf16[432,1024]{1,0:T(8,128)(2,1)S(1)}, bf16[432,1024]{1,0:T(8,128)(2,1)}, u32[]{:S(2)}) copy-start(bf16[432,1024]{1,0:T(8,128)(2,1)} %param.9) | copy-start | bytes 2654212
  13.7 200.7 %all-to-all-start = ((bf16[4,512,1024]{2,1,0:T(8,128)(2,1)}), bf16[4,512,1024]{2,1,0:T(8,128)(2,1)}, u32[]{:S(2)}, u32[]{:S(2)}) async-start(bf16[4,512,1024]{2,1,0:T(8,128)(2,1)} %broadcast_in_dim.46), calls=%async_computation | async-start | bytes 8388608 | tf_op jit(solution)/shard_map/all_to_all | solution.py:26
  84.1 127.7 %collective-permute-start = (s32[512]{0:T(512)S(1)}, s32[512]{0:T(512)S(1)}, u32[]{:S(2)}, u32[]{:S(2)}) collective-permute-start(s32[512]{0:T(512)S(1)} %copy-done.6), channel_id=1, source_target_pairs={{0,0},{1,1},{2,32},{3,33},{4,64},{5,65},{6,96},{7,97},{8,2},{9,3},... | collective-permute-start | bytes 6152 | tf_op jit(solution)/shard_map/ppermute | solution.py:44
  210.0 0.9 copy-start.2
  394.8 63.6 %all-to-all-start.1 = ((f32[4,128,1728]{1,2,0:T(8,128)}), f32[4,128,1728]{1,2,0:T(8,128)S(1)}, u32[]{:S(2)}, u32[]{:S(2)}) async-start(f32[4,128,1728]{1,2,0:T(8,128)} %bitcast.29), calls=%async_computation.1 | async-start | bytes 7077888 | tf_op jit(solution)/shard_map/all_to_all | solution.py:71
  421.3 39.8 %copy-start.3 = (f32[1728]{0:T(1024)S(1)}, f32[1728]{0:T(1024)}, u32[]{:S(2)}) copy-start(f32[1728]{0:T(1024)} %eq.79) | copy-start | bytes 20740
  461.1 52.0 %copy-start = (bf16[512,1024]{1,0:T(8,128)(2,1)S(1)}, bf16[512,1024]{1,0:T(8,128)(2,1)}, u32[]{:S(2)}) copy-start(bf16[512,1024]{1,0:T(8,128)(2,1)} %param.8) | copy-start | bytes 3145732
  478.5 0.7 collective-permute-start.2
  514.8 20.9 %all-to-all-start.4 = ((f32[16,16,1024]{2,1,0:T(8,128)}), f32[16,16,1024]{2,1,0:T(8,128)S(1)}, u32[]{:S(2)}, u32[]{:S(2)}) async-start(f32[16,16,1024]{2,1,0:T(8,128)} %pad_maximum_fusion), calls=%async_computation.4 | async-start | bytes 2097152 | tf_op jit(solution)/shard_map/all_to_all | solution.py:96
Sparse Core Ops, SparseCore 0:
  9.8 365.1 all-gather.3
